TPU v7x, 256 devices: a whole 4x4x8 slice. The times are simulated.
256 devices in a mesh: seq: 64 (over x, z, core), head: 4 (over y).
Axes of the slice: x: 4, y: 4, z: 8, core: 2. Of those that a mesh axis runs over, the one named last changes fastest.
Arguments:
- feat_q: bfloat16 [65536, 256], P('seq', 'head'), may hold values from -6 to 6
- feat_k: bfloat16 [65536, 256], P('seq', 'head'), may hold values from -6 to 6
- values: bfloat16 [65536, 2048], P('seq', 'head'), may hold values from -6 to 6
- win_q: bfloat16 [65536, 2048], P('seq', 'head'), may hold values from -6 to 6
- win_k: bfloat16 [65536, 2048], P('seq', 'head'), may hold values from -6 to 6
- win_v: bfloat16 [65536, 2048], P('seq', 'head'), may hold values from -6 to 6
- head_gain: float32 [16], P('head'), may hold values from 0.8 to 3.8
Outputs:
- mixed: bfloat16 [65536, 2048], P('seq', 'head')
All inputs are finite; a program needn't handle non-finite values.
Results may differ from a plain program's by a relative error of at most 0.0032.
Values may be sent and summed in bfloat16 or wider, within the bound.
A program may use at most 128 MiB of HBM per device.

v0:
```python
import math

import jax
import jax.numpy as jnp
from jax import lax
from jax.sharding import PartitionSpec as P

W = 64
BLOCK = 512


quad_scale = 1.0 / (4.0 * math.sqrt(2.0))
eps = 1e-06
highest_setting = lax.Precision.HIGHEST


def entering(value, axis, join, neutral):
    count, mine = (lax.axis_size(axis), lax.axis_index(axis))
    pieces = jax.tree.map(lambda part: lax.all_gather(part, axis), value)
    subtotal = jax.tree.map(
        lambda part, zero: jnp.full_like(part, 0) + jnp.asarray(zero, part.dtype), value, neutral
    )

    def lap(position, subtotal):
        longer = join(subtotal, jax.tree.map(lambda part: part[position], pieces))
        return jax.tree.map(lambda new, old: jnp.where(position < mine, new, old), longer, subtotal)

    return lax.fori_loop(0, count - 1, lap, subtotal)


def shifted(value, axis, steps):
    count = lax.axis_size(axis)
    leading, last = (max(0, -steps), min(count, count - steps))
    return lax.ppermute(value, axis, [(source, source + steps) for source in range(leading, last)])


def feature_map(inputs):
    widened = inputs.astype(jnp.float32)
    feat_size = widened.shape[-1]
    quadratic = (widened[..., :, None] * widened[..., None, :]).reshape(
        widened.shape[:-1] + (feat_size * feat_size,)
    ) * quad_scale
    constant = jnp.ones(widened.shape[:-1] + (1,), jnp.float32)
    mapped = jnp.concatenate([constant, widened * 0.5, quadratic], axis=-1).astype(jnp.bfloat16)
    return mapped


def add_states(earlier, later):
    return (earlier[0] + later[0], earlier[1] + later[1])


def local(feat_q, feat_k, values, win_q, win_k, win_v, head_gain):
    tok_rows = values.shape[0]
    head_count = head_gain.shape[0]
    head_size = values.shape[1] // head_count
    feat_size = feat_q.shape[1] // head_count
    query_features = feat_q.reshape(tok_rows, head_count, feat_size)
    key_features = feat_k.reshape(tok_rows, head_count, feat_size)
    map_q = feature_map(query_features)
    mapped_keys = feature_map(key_features)
    value_rows = values.reshape(tok_rows, head_count, head_size)
    block_count = tok_rows // BLOCK
    block_states = []
    block_normals = []
    for block in range(block_count):
        covered_rows = slice(block * BLOCK, (block + 1) * BLOCK)
        block_states.append(
            jnp.einsum(
                "rlb,rlg->lbg",
                mapped_keys[covered_rows],
                value_rows[covered_rows],
                preferred_element_type=jnp.float32,
            )
        )
        block_normals.append(jnp.sum(mapped_keys[covered_rows].astype(jnp.float32), axis=0))
    shard_state = block_states[0]
    shard_normal = block_normals[0]
    block = 1
    shard_state = shard_state + block_states[block]
    shard_normal = shard_normal + block_normals[block]
    empty = (jnp.zeros_like(shard_state), jnp.zeros_like(shard_normal))
    run_state, run_normal = entering((shard_state, shard_normal), "seq", add_states, empty)
    edge_k, edge_v = shifted((win_k[tok_rows - W :], win_v[tok_rows - W :]), "seq", 1)
    ext_k = jnp.concatenate([edge_k, win_k], axis=0).reshape(tok_rows + W, head_count, head_size)
    ext_v = jnp.concatenate([edge_v, win_v], axis=0).reshape(tok_rows + W, head_count, head_size)
    queries = win_q.reshape(tok_rows, head_count, head_size)
    anchor = lax.axis_index("seq") * tok_rows
    row_ids = jnp.arange(BLOCK, dtype=jnp.int32)[:, None]
    col_ids = jnp.arange(BLOCK + W, dtype=jnp.int32)[None, :]
    causal = row_ids >= jnp.arange(BLOCK, dtype=jnp.int32)[None, :]
    band = (col_ids <= row_ids + W) & (col_ids > row_ids)
    gains = head_gain[None, :, None]
    pieces = []
    for block in range(block_count):
        covered_rows = slice(block * BLOCK, (block + 1) * BLOCK)
        common_range = jnp.einsum(
            "cau,bau->acb",
            query_features[covered_rows],
            key_features[covered_rows],
            preferred_element_type=jnp.float32,
        )
        kernel = jnp.where(
            causal[None], 1.0 + common_range * 0.25 + common_range * common_range / 32.0, 0.0
        ).astype(jnp.bfloat16)
        block_map = map_q[covered_rows].astype(jnp.float32)
        numer = jnp.einsum(
            "hqk,khd->qhd", kernel, value_rows[covered_rows], preferred_element_type=jnp.float32
        )
        numer = numer + jnp.einsum("qhf,hfd->qhd", block_map, run_state, precision=highest_setting)
        denom = jnp.sum(kernel.astype(jnp.float32), axis=2).T + jnp.einsum(
            "qhf,hf->qh", block_map, run_normal, precision=highest_setting
        )
        linear = numer / denom[..., None]
        run_state = run_state + block_states[block]
        run_normal = run_normal + block_normals[block]
        keys = ext_k[block * BLOCK : block * BLOCK + BLOCK + W]
        wvals = ext_v[block * BLOCK : block * BLOCK + BLOCK + W]
        scores = jnp.einsum(
            "qhd,khd->hqk", queries[covered_rows], keys, preferred_element_type=jnp.float32
        ) / math.sqrt(head_size)
        valid = band & (anchor + block * BLOCK - W + col_ids >= 0)
        scores = jnp.where(valid[None], scores, -1e30)
        peak = jnp.max(scores, axis=2, keepdims=True)
        weights = jnp.exp(scores - peak)
        weights = (weights / jnp.sum(weights, axis=2, keepdims=True)).astype(jnp.bfloat16)
        window = jnp.einsum("hqk,khd->qhd", weights, wvals, preferred_element_type=jnp.float32)
        pieces.append(gains * (linear + window))
    combined = jnp.concatenate(pieces, axis=0).reshape(tok_rows, head_count * head_size)
    squares = lax.psum(jnp.sum(combined * combined, axis=1), "head")
    power = squares / (head_count * head_size * lax.axis_size("head"))
    return (combined * lax.rsqrt(power + eps)[:, None]).astype(jnp.bfloat16)


def solution(mesh):
    placed = (
        P("seq", "head"),
        P("seq", "head"),
        P("seq", "head"),
        P("seq", "head"),
        P("seq", "head"),
        P("seq", "head"),
        P("head"),
    )
    return jax.shard_map(
        local, mesh=mesh, in_specs=placed, out_specs=P("seq", "head"), check_vma=False
    )
```

profile of v0, /device:TPU:1, one launch (start us, length us, event | category | flops | bytes accessed | tf_op | source)
XLA Modules:
  0.0 283.5 jit_solution(13005787981981457901)
XLA Ops:
  7.6 1.7 multiply_convert_fusion.2
  10.2 1.9 multiply_convert_fusion
  12.1 1.9 multiply_convert_fusion.1
  14.5 4.5 %pad_maximum_fusion = (bf16[1024,4,273]{0,2,1:T(8,128)(2,1)S(1)}, bf16[1024,4,273]{0,2,1:T(8,128)(2,1)}) fusion(bf16[1024,4,256]{0,2,1:T(8,128)(2,1)} %bitcast.118, bf16[1024,4,16]{0,2,1:T(8,128)(2,1)} %get-tuple-element.181, bf16[273]{0:T(512)(128)(2,1)S(1)} %pad.9.clone, bf16[1024,4,256]{0,2,1:T(8,128)(2,1)} %bitcast.117, ...), kind=kLoop, calls=%fused_computation.26 | loop fusion | flops 12300288 | bytes 8929826 | tf_op jit(solution)/shard_map/concatenate | solution.py:44
  20.3 1.3 convolution_add_fusion
  21.6 1.5 slice.110
  23.1 4.9 %collective-permute-start.1 = (bf16[64,512]{1,0:T(8,128)(2,1)}, bf16[64,512]{1,0:T(8,128)(2,1)}, u32[]{:S(2)}, u32[]{:S(2)}) collective-permute-start(bf16[64,512]{1,0:T(8,128)(2,1)} %slice.110), channel_id=1, source_target_pairs={{0,4},{4,8},{8,12},{12,16},{16,20},{20,24},{24,28},{28,32},{32,36}... | collective-permute-start | bytes 196616 | tf_op jit(solution)/shard_map/ppermute | solution.py:34
  28.1 1.5 slice.107
  29.5 1.9 collective-permute-start
  31.5 2.3 fusion.56
  33.7 2.1 copy.72
  35.8 2.0 copy.73
  39.8 1.5 convert_reduce_fusion.1
  41.3 1.9 convolution_bitcast_fusion.1
  43.2 1.5 convert_reduce_fusion
  44.7 1.9 convolution_bitcast_fusion
  46.6 51.7 %all-gather.2 = f32[64,4,273]{2,1,0:T(4,128)S(1)} all-gather(f32[1,4,273]{2,1,0:T(4,128)S(1)} %add_bitcast_fusion.1), channel_id=3, replica_groups=mesh['seq'=64,'head'=4] {'seq'}, dimensions={0}, use_global_device_ids=true | all-gather | bytes 283920 | tf_op jit(solution)/shard_map/all_gather | solution.py:19
  102.0 2.6 fusion.61
  104.7 2.6 fusion.60
  107.3 2.1 fusion.14
  109.4 2.1 fusion.13
  111.5 65.2 %all-gather.5.cloned.1.call-done = f32[256,273,128]{2,1,0:T(8,128)} async-done(((f32[4,273,128]{2,1,0:T(8,128)}), f32[256,273,128]{2,1,0:T(8,128)}) %all-gather.5.cloned.1.call-update) | async-done | bytes 35782672 | tf_op jit(solution)/shard_map/all_gather | solution.py:19
  176.7 79.6 %while.16 = (s32[]{:T(128)}, f32[4,273,128]{2,1,0:T(8,128)S(1)}, f32[4,273]{1,0:T(4,128)S(1)}, s32[]{:T(128)}, f32[64,4,273,128]{3,2,1,0:T(8,128)}, /*index=5*/f32[64,4,273]{2,1,0:T(4,128)S(1)}, s32[]{:T(128)}, s32[]{:T(128)}) while((s32[]{:T(128)}, f32[4,273,128]{2,1,0:T(8,128)S(1)}, f32[4,273]{1,0:T(4,128)S(1)}, s32[]{:T(128)}, ...), condition=%wide.region_3.4_spmd.clone, body=%wide.region_2.3_spmd.clone.sunk | while | flops 422608 | bytes 1690531 | solution.py:28
  176.7 1.2 add_select_fusion.4
  178.0 1.2 add_select_fusion.4
  179.2 1.2 add_select_fusion.4
  180.5 1.2 add_select_fusion.4
  181.8 1.2 add_select_fusion.4
  183.0 1.2 add_select_fusion.4
  184.3 1.2 add_select_fusion.4
  185.6 1.2 add_select_fusion.4
  186.8 1.2 add_select_fusion.4
  188.1 1.2 add_select_fusion.4
  189.3 1.2 add_select_fusion.4
  190.6 1.2 add_select_fusion.4
  191.9 1.2 add_select_fusion.4
  193.1 1.2 add_select_fusion.4
  194.4 1.2 add_select_fusion.4
  195.7 1.2 add_select_fusion.4
  200.7 1.2 add_select_fusion.4
  202.0 1.2 add_select_fusion.4
  207.0 1.2 add_select_fusion.4
  208.3 1.2 add_select_fusion.4
  212.1 1.2 add_select_fusion.4
  213.4 1.2 add_select_fusion.4
  218.4 1.2 add_select_fusion.4
  219.7 1.2 add_select_fusion.4
  224.7 1.2 add_select_fusion.4
  226.0 1.2 add_select_fusion.4
  231.1 1.2 add_select_fusion.4
  232.3 1.2 add_select_fusion.4
  236.1 1.2 add_select_fusion.4
  237.4 1.2 add_select_fusion.4
  242.4 1.2 add_select_fusion.4
  243.7 1.2 add_select_fusion.4
  248.7 1.2 add_select_fusion.4
  250.0 1.2 add_select_fusion.4
  255.1 1.2 add_select_fusion.4
  257.7 3.3 %fusion.22 = f32[512,4,128]{2,0,1:T(8,128)S(1)} fusion(f32[512,4,128]{2,0,1:T(8,128)} %fusion.14, f32[512,4,128]{2,0,1:T(8,128)} %convolution_bitcast_fusion.1, f32[4,273,128]{2,1,0:T(8,128)S(1)} %get-tuple-element.115, bf16[1024,4,273]{0,2,1:T(8,128)(2,1)S(1)} %copy-done, f32[512,4]{0,1:T(4,128)S(1)} %fusion.49, f32[4]{0:T(128)S(1)} %copy-done.12), kind=kOutput, calls=%fused_computation.47 | convolution fusion | flops 859832320 | bytes 4874752 | tf_op jit(solution)/shard_map/qhf,hfd->qhd/dot_general | solution.py:109
  261.1 1.8 fusion.18
  263.2 1.9 copy.53
  265.1 8.4 %psum.7 = f32[1024]{0:T(1024)S(1)} all-reduce(f32[1024]{0:T(1024)S(1)} %get-tuple-element.152), channel_id=1, replica_groups=mesh['seq'=64,'head'=4] {'head'}, use_global_device_ids=true, to_apply=%region_11.12 | all-reduce | flops 1024 | bytes 8192 | tf_op jit(solution)/shard_map/psum | solution.py:129
  273.5 1.8 fusion.12
  275.4 1.3 copy.54
  (151 shorter events, 46.2 us)
Async XLA Ops:
  6.5 7.5 %copy-start.9 = (bf16[1024,512]{1,0:T(8,128)(2,1)S(1)}, bf16[1024,512]{1,0:T(8,128)(2,1)}, u32[]{:S(2)}) copy-start(bf16[1024,512]{1,0:T(8,128)(2,1)} %param.11) | copy-start | bytes 3145732
  6.5 170.2 %all-gather.5.cloned.1.call-start = ((), (), s32[]{:S(2)}) async-start(), calls=%async_computation | async-start | bytes 37273600 | tf_op jit(solution)/shard_map/all_gather | solution.py:19
  14.3 4.7 %copy-start.3 = (bf16[512,512]{0,1:T(8,128)(2,1)}, bf16[512,512]{0,1:T(8,128)(2,1)S(1)}, u32[]{:S(2)}) copy-start(bf16[512,512]{0,1:T(8,128)(2,1)S(1)} %copy.70) | copy-start | bytes 1572868
  19.5 0.8 copy-start.10
  21.6 16.9 %copy-start.7 = (bf16[1024,64]{0,1:T(8,128)(2,1)S(1)}, bf16[1024,64]{0,1:T(8,128)(2,1)}, u32[]{:S(2)}) copy-start(bf16[1024,64]{0,1:T(8,128)(2,1)} %param.9) | copy-start | bytes 393220
  23.1 75.2 %collective-permute-start.1 = (bf16[64,512]{1,0:T(8,128)(2,1)}, bf16[64,512]{1,0:T(8,128)(2,1)}, u32[]{:S(2)}, u32[]{:S(2)}) collective-permute-start(bf16[64,512]{1,0:T(8,128)(2,1)} %slice.110), channel_id=1, source_target_pairs={{0,4},{4,8},{8,12},{12,16},{16,20},{20,24},{24,28},{28,32},{32,36}... | collective-permute-start | bytes 196616 | tf_op jit(solution)/shard_map/ppermute | solution.py:34
  29.5 69.9 %collective-permute-start = (bf16[64,512]{1,0:T(8,128)(2,1)}, bf16[64,512]{1,0:T(8,128)(2,1)}, u32[]{:S(2)}, u32[]{:S(2)}) collective-permute-start(bf16[64,512]{1,0:T(8,128)(2,1)} %slice.107), channel_id=1, source_target_pairs={{0,4},{4,8},{8,12},{12,16},{16,20},{20,24},{24,28},{28,32},{32,36}... | collective-permute-start | bytes 196616 | tf_op jit(solution)/shard_map/ppermute | solution.py:34
  39.8 1.5 copy-start.4
  44.7 53.6 %copy-start.1 = (bf16[1024,512]{1,0:T(8,128)(2,1)S(1)}, bf16[1024,512]{1,0:T(8,128)(2,1)}, u32[]{:S(2)}) copy-start(bf16[1024,512]{1,0:T(8,128)(2,1)} %param.13) | copy-start | bytes 3145732
  44.7 54.7 %copy-start.2 = (bf16[1024,512]{1,0:T(8,128)(2,1)S(1)}, bf16[1024,512]{1,0:T(8,128)(2,1)}, u32[]{:S(2)}) copy-start(bf16[1024,512]{1,0:T(8,128)(2,1)} %param.14) | copy-start | bytes 3145732
  44.7 55.8 %copy-start.6 = (bf16[512,512]{0,1:T(8,128)(2,1)S(1)}, bf16[512,512]{0,1:T(8,128)(2,1)}, u32[]{:S(2)}) copy-start(bf16[512,512]{0,1:T(8,128)(2,1)} %copy.72) | copy-start | bytes 1572868
  99.4 1.9 copy-start.5
  109.4 147.0 %copy-start = (bf16[1024,4,273]{0,2,1:T(8,128)(2,1)S(1)}, bf16[1024,4,273]{0,2,1:T(8,128)(2,1)}, u32[]{:S(2)}) copy-start(bf16[1024,4,273]{0,2,1:T(8,128)(2,1)} %get-tuple-element.169) | copy-start | bytes 6709252
  176.7 81.0 %copy-start.12 = (f32[4]{0:T(128)S(1)}, f32[4]{0:T(128)}, u32[]{:S(2)}) copy-start(f32[4]{0:T(128)} %param.15) | copy-start | bytes 52
  256.3 4.7 %copy-start.8 = (f32[512,4,128]{2,0,1:T(8,128)S(1)}, f32[512,4,128]{2,0,1:T(8,128)}, u32[]{:S(2)}) copy-start(f32[512,4,128]{2,0,1:T(8,128)} %convolution_bitcast_fusion) | copy-start | bytes 3145732
  256.3 4.7 %copy-start.11 = (f32[4,273,128]{2,1,0:T(8,128)S(1)}, f32[4,273,128]{2,1,0:T(8,128)}, u32[]{:S(2)}) copy-start(f32[4,273,128]{2,1,0:T(8,128)} %copy-done.10) | copy-start | bytes 1677316
  256.3 4.7 %copy-start.13 = (f32[512,4,128]{2,0,1:T(8,128)S(1)}, f32[512,4,128]{2,0,1:T(8,128)}, u32[]{:S(2)}) copy-start(f32[512,4,128]{2,0,1:T(8,128)} %fusion.13) | copy-start | bytes 3145732
Sparse Core Ops, SparseCore 0:
  21.8 154.9 all-gather.4
where the time goes:
time: 287 us; the launch traced here: 284 us
  other arithmetic  100 us (35%)
  waiting for transfers between devices  65.3 us (23%)
  blocking collectives  60.1 us (21%)
  matrix products  20.7 us (7%)
  local copies, waits for them, and re-layouts  14.8 us (5%)
  between operations  13.8 us (5%)
  starting transfers between devices  6.84 us (2%)
    select_n x126, other arithmetic, lap(): jnp.where(position < mine, new, old)  77.9 us
    all_gather x1, waiting for transfers between devices, entering(): pieces = jax.tree.map(lambda part: lax.all_gather(part, axis), value)  65.2 us
    all_gather x1, blocking collectives, entering(): pieces = jax.tree.map(lambda part: lax.all_gather(part, axis), value)  51.7 us
    psum x1, blocking collectives, local(): squares = lax.psum(jnp.sum(combined * combined, axis=1), 'head')  8.42 us
    ppermute x2, starting transfers between devices, shifted(): lax.ppermute(value, axis, [(source, source + steps) for source in range(l...  6.83 us
  transfers between devices with their start and end apart: 3, of which 1 were waited for; matrix products, arithmetic and copies ran while one was open for 11% of the time, Pallas kernels for 0%

commit v1 on v0

v1 whole, which is shorter than its diff:
```python
import functools
import math

import jax
import jax.numpy as jnp
import numpy as np
from jax import lax
from jax.experimental import pallas as pl
from jax.experimental.pallas import tpu as pltpu
from jax.sharding import PartitionSpec as P

MESH = pl.DeviceIdType.MESH
F32 = jnp.float32
BF16 = jnp.bfloat16

W = 64
BLOCK = 512
FEAT = 16
HD = 128
ROWS = 160
PIECE = 16
QUAD = 1.0 / (4.0 * math.sqrt(2.0))
EPS = 1e-06


def feature_tables(heads):
    ones_lane = heads * FEAT
    first = np.zeros((heads, ROWS, 128), np.float32)
    second = np.zeros((heads, ROWS, 128), np.float32)
    scale_k = np.zeros((ROWS,), np.float32)
    scale_q = np.zeros((ROWS,), np.float32)
    row = 0
    for shift in range(FEAT // 2 + 1):
        for a in range(FEAT if shift < FEAT // 2 else FEAT // 2):
            for h in range(heads):
                first[h, row, h * FEAT + a] = 1.0
                second[h, row, h * FEAT + (a + shift) % FEAT] = 1.0
            scale_k[row] = QUAD
            scale_q[row] = np.float32(QUAD) * (1.0 if shift == 0 else 2.0)
            row += 1
    for a in range(FEAT):
        for h in range(heads):
            first[h, row, h * FEAT + a] = 1.0
            second[h, row, ones_lane] = 1.0
        scale_k[row] = scale_q[row] = 0.5
        row += 1
    first[:, row, ones_lane] = 1.0
    second[:, row, ones_lane] = 1.0
    scale_k[row] = scale_q[row] = 1.0
    row += 1
    assert row + 2 <= ROWS
    wide_k = np.broadcast_to(scale_k[:, None], (ROWS, 128))
    wide_q = np.broadcast_to(scale_q[None, :], (8, ROWS))
    return first, second, np.ascontiguousarray(wide_k), np.ascontiguousarray(wide_q), row


def dot(a, b):
    return jnp.dot(a, b, preferred_element_type=F32)


def dot_nt(a, b):
    return lax.dot_general(a, b, (((1,), (1,)), ((), ())), preferred_element_type=F32)


def split(x):
    high = x.astype(BF16)
    return high, (x - high.astype(F32)).astype(BF16)


def mixer(
    dims,
    fq_hbm, fk_hbm, v_hbm, wq_hbm, wk_hbm, wv_hbm, gain, ea_hbm, eb_hbm, sk_hbm, sq_hbm,
    out_hbm,
    fq, fk, v, wq, wk, wv, ea, eb, sk, sq,
    edge_k, edge_v, first_state, total, got, chip_sum, gathered, prefixes, arrived, payload, before,
    local, window, map_q, power_own, power_all, squares, out,
    in_sem, out_sem, send_sem, recv_sem,
):
    seq_n, head_n, z_n, heads, tokens, normal_row = dims
    chips = seq_n // 2
    half = heads // 2
    pieces = half * ROWS // PIECE
    blocks = tokens // BLOCK
    me, head = lax.axis_index("seq"), lax.axis_index("head")
    core = lax.rem(me, 2)
    chip = me // 2
    other = me + 1 - 2 * core

    def load(index, src, dst):
        return pltpu.make_async_copy(src, dst, in_sem.at[index])

    loads = [
        load(0, fk_hbm, fk),
        load(1, ea_hbm, ea), load(2, eb_hbm, eb), load(3, sk_hbm, sk),
        load(4, v_hbm, v), load(5, fq_hbm, fq), load(6, sq_hbm, sq),
        load(7, wk_hbm, wk), load(8, wq_hbm, wq), load(9, wv_hbm, wv),
    ]
    for copy in loads:
        copy.start()

    def remote(src, dst, index, seq, group):
        return pltpu.make_async_remote_copy(
            src_ref=src, dst_ref=dst, send_sem=send_sem.at[index], recv_sem=recv_sem.at[index],
            device_id=(seq, group), device_id_type=MESH,
        )

    def settle(buffer, count, sem):
        pltpu.make_async_copy(buffer.at[pl.ds(0, count)], buffer.at[pl.ds(0, count)], sem).wait()

    barrier = pltpu.get_barrier_semaphore()
    edge_mate = lax.rem(me + 2 * core - 1 + seq_n, seq_n)

    def greet(seq, group):
        pl.semaphore_signal(barrier, inc=1, device_id=(seq, group), device_id_type=MESH)

    greet(other, head)
    greet(edge_mate, head)
    for step in range(1, head_n):
        greet(me, lax.rem(head + step, head_n))

    def greet_chip(step, carry):
        greet(2 * lax.rem(chip + step, chips) + core, head)
        return carry

    lax.fori_loop(1, chips, greet_chip, 0)

    lanes = lax.broadcasted_iota(jnp.int32, (128, 128), 1)
    subs = lax.broadcasted_iota(jnp.int32, (128, 128), 0)
    eye = lanes == subs
    ones_v = jnp.ones((BLOCK, HD), BF16)
    tail = jnp.where(lax.broadcasted_iota(jnp.int32, (BLOCK, 128 - heads * FEAT), 1) == 0, 1.0, 0.0).astype(BF16)
    for index in range(4):
        loads[index].wait()
    loads[4].wait()

    def with_one(ref, start):
        return jnp.concatenate([ref[pl.ds(start, BLOCK), :], tail], axis=1)

    def state_of(h):
        cols = pl.ds(pl.multiple_of(h * HD, HD), HD)
        summed = None
        for block in range(blocks):
            keys = with_one(fk, block * BLOCK)
            scale = sk[...]
            mapped = dot_nt(ea[h], keys) * dot_nt(eb[h], keys)
            mapped = (mapped * jnp.concatenate([scale] * (BLOCK // 128), axis=1)).astype(BF16)
            both = dot(mapped, jnp.concatenate([v[pl.ds(block * BLOCK, BLOCK), cols], ones_v], axis=1))
            state, normal = both[:, :HD], both[:, HD:]
            low = jnp.sum(jnp.where(eye, normal[:128], 0.0), axis=0, keepdims=True)
            high = jnp.sum(jnp.where(eye[: ROWS - 128], normal[128:], 0.0), axis=0, keepdims=True)
            row_ids = lax.broadcasted_iota(jnp.int32, (ROWS, HD), 0)
            state = jnp.where(row_ids == normal_row, low, jnp.where(row_ids == normal_row + 1, high, state))
            if block == 0:
                first_state[h] = state
            summed = state if summed is None else summed + state
        per_head = ROWS // PIECE
        total[pl.ds(h * per_head, per_head)] = summed.reshape(per_head, PIECE, HD)

    def states(start):
        def body(i, carry):
            state_of(start + i)
            return carry
        lax.fori_loop(0, half, body, 0)

    states(half * (1 - core))
    pl.semaphore_wait(barrier, 1 + 1 + head_n - 1 + chips - 1)
    swap_out = remote(total.at[pl.ds((1 - core) * pieces, pieces)], got, 0, other, head)
    swap_out.start()
    states(half * core)

    following = lax.rem(me + 1, seq_n)
    edges = [
        remote(wk_hbm.at[pl.ds(tokens - W, W)], edge_k, 1, following, head),
        remote(wv_hbm.at[pl.ds(tokens - W, W)], edge_v, 2, following, head),
    ]
    for copy in edges:
        copy.start()
    swap_out.wait_recv()
    own = pl.ds(core * pieces, pieces)
    chip_sum[...] = total[own] + got[...]

    def owner_chip(k):
        return lax.rem(k, chips // z_n) * z_n + k // (chips // z_n)

    owned = lax.rem(chip, z_n) * (chips // z_n) + chip // z_n
    is_owner = owned < pieces

    def send_piece(i, carry):
        k = lax.rem(owned + i, pieces)

        @pl.when(owner_chip(k) != chip)
        def _():
            remote(chip_sum.at[k], gathered.at[chip], 3, 2 * owner_chip(k) + core, head).start()
        return carry

    lax.fori_loop(0, pieces, send_piece, 0)

    for index in (5, 6, 7, 8, 9):
        loads[index].wait()
    quarter = BLOCK // 2
    tri = lax.broadcasted_iota(jnp.int32, (quarter, quarter), 0) >= lax.broadcasted_iota(jnp.int32, (quarter, quarter), 1)
    feat_lane = lax.broadcasted_iota(jnp.int32, (1, heads * FEAT), 1)

    def within(i, carry):
        h, block = i // blocks, lax.rem(i, blocks)
        cols = pl.ds(pl.multiple_of(h * HD, HD), HD)
        start = pl.multiple_of(block * BLOCK, BLOCK)
        keys = fk[pl.ds(start, BLOCK), :]
        mine = jnp.where(feat_lane // FEAT == h, 1.0, 0.0).astype(BF16)
        queries = fq[pl.ds(start, BLOCK), :] * mine
        vals = jnp.concatenate([v[pl.ds(start, BLOCK), cols], ones_v], axis=1)

        def weights(q, k):
            s = dot_nt(q, k)
            return 1.0 + s * 0.25 + s * s * (1.0 / 32.0)

        top = jnp.where(tri, weights(queries[:quarter], keys[:quarter]), 0.0).astype(BF16)
        local[h, pl.ds(start, quarter), :] = dot(top, vals[:quarter])
        left = weights(queries[quarter:], keys[:quarter]).astype(BF16)
        right = jnp.where(tri, weights(queries[quarter:], keys[quarter:]), 0.0).astype(BF16)
        local[h, pl.ds(start + quarter, quarter), :] = dot(jnp.concatenate([left, right], axis=1), vals)
        ext = with_one(fq, start)
        mapped = dot_nt(ext, ea[h]) * dot_nt(ext, eb[h]) * sq[0:1, :]
        map_q[h, pl.ds(start, BLOCK), :] = mapped.astype(BF16)
        return carry

    lax.fori_loop(0, heads * blocks, within, 0)

    band_row = lax.broadcasted_iota(jnp.int32, (W, 2 * W), 0)
    band_col = lax.broadcasted_iota(jnp.int32, (W, 2 * W), 1)
    band = (band_col > band_row) & (band_col <= band_row + W)
    sharp = 1.0 / math.sqrt(HD)

    def attend(scores, allowed):
        scores = jnp.where(allowed, scores * sharp, -1e30)
        weights = jnp.exp(scores - jnp.max(scores, axis=1, keepdims=True))
        return (weights / jnp.sum(weights, axis=1, keepdims=True)).astype(BF16)

    group = 4
    band_group = jnp.concatenate([band] * group, axis=0)

    def windows(h, first, count):
        cols = pl.ds(pl.multiple_of(h * HD, HD), HD)
        starts = [first + c * W for c in range(count)]
        scores = [
            dot_nt(wq[pl.ds(s, W), cols], wk[pl.ds(s - W, 2 * W), cols]) for s in starts
        ]
        probs = attend(jnp.concatenate(scores, axis=0), band_group[: count * W])
        for c, s in enumerate(starts):
            window[pl.ds(s, W), cols] = dot(probs[c * W : (c + 1) * W], wv[pl.ds(s - W, 2 * W), cols])

    def window_head(h, carry):
        windows(h, W, group - 1)

        def rest(g, inner):
            windows(h, pl.multiple_of(g * group * W, group * W), group)
            return inner

        return lax.fori_loop(1, tokens // (group * W), rest, carry)

    lax.fori_loop(0, heads, window_head, 0)

    edges[0].wait_recv()
    edges[1].wait_recv()
    band_first = band & ((band_col >= W) | (me > 0))

    def window_edge(h, carry):
        cols = pl.ds(pl.multiple_of(h * HD, HD), HD)
        keys = jnp.concatenate([edge_k[:, cols], wk[pl.ds(0, W), cols]], axis=0)
        vals = jnp.concatenate([edge_v[:, cols], wv[pl.ds(0, W), cols]], axis=0)
        probs = attend(dot_nt(wq[pl.ds(0, W), cols], keys), band_first)
        window[pl.ds(0, W), cols] = dot(probs, vals)
        return carry

    lax.fori_loop(0, heads, window_edge, 0)

    @pl.when(is_owner)
    def _():
        gathered[chip] = chip_sum[owned]
        settle(gathered, chips - 1, recv_sem.at[3])

        def add(u, run):
            prefixes[u] = run
            return run + gathered[u]

        lax.fori_loop(0, chips, add, jnp.zeros((PIECE, HD), F32))

        def send_prefix(i, carry):
            u = lax.rem(chip + i, chips)
            remote(prefixes.at[u], arrived.at[owned], 4, 2 * u + core, head).start()
            return carry

        lax.fori_loop(1, chips, send_prefix, 0)
        arrived[owned] = prefixes[chip]
        settle(arrived, pieces - 1, recv_sem.at[4])

    @pl.when(jnp.logical_not(is_owner))
    def _():
        settle(arrived, pieces, recv_sem.at[4])

    ahead = jnp.where(core == 0, 1.0, 0.0)
    payload[...] = arrived[...] + total[own] * ahead
    swap_back = remote(payload, before.at[own], 5, other, head)
    swap_back.start()
    before[own] = arrived[...] + got[...] * (1.0 - ahead)

    per_head = ROWS // PIECE

    def finish(h, block, fresh):
        cols = pl.ds(pl.multiple_of(h * HD, HD), HD)
        rows = pl.ds(block * BLOCK, BLOCK)
        state = before[pl.ds(h * per_head, per_head)].reshape(ROWS, HD)
        if block > 0:
            state = state + first_state[h]
        normal = jnp.concatenate(
            [
                jnp.broadcast_to(state[normal_row : normal_row + 1], (HD, HD)).T,
                jnp.broadcast_to(state[normal_row + 1 : normal_row + 2], (HD, HD)).T[: ROWS - HD],
            ],
            axis=0,
        )
        high, low = split(jnp.concatenate([state, normal], axis=1))
        mapped = map_q[h, rows, :]
        sums = dot(mapped, high) + dot(mapped, low) + local[h, rows, :]
        combined = gain[h] * (sums[:, :HD] / sums[:, HD:] + window[rows, cols])
        window[rows, cols] = combined
        squared = combined * combined
        squares[rows, :] = squared if fresh else squares[rows, :] + squared

    own_head = half * core
    for block in range(blocks):
        finish(own_head, block, True)
    for i in range(1, half):
        for block in range(blocks):
            finish(own_head + i, block, False)
    swap_back.wait_recv()
    for block in range(blocks):
        for i in range(half):
            finish(half * (1 - core) + i, block, False)
        sums = jnp.sum(squares[pl.ds(block * BLOCK, BLOCK), :], axis=1, keepdims=True)
        for r in range(BLOCK // 128):
            wide = jnp.broadcast_to(sums[r * 128 : (r + 1) * 128], (128, 128))
            power_own[block, r : r + 1, :] = jnp.sum(jnp.where(eye, wide, 0.0), axis=0, keepdims=True)
        power_all[block, head] = power_own[block]
        for step in range(1, head_n):
            remote(
                power_own.at[block], power_all.at[block, head], 6 + block, me, lax.rem(head + step, head_n)
            ).start()

    stores = []
    for block in range(blocks):
        rows = pl.ds(block * BLOCK, BLOCK)
        settle(power_all.at[block], head_n - 1, recv_sem.at[6 + block])
        power = jnp.sum(power_all[block], axis=0) * (1.0 / (heads * head_n * HD))
        factor = lax.rsqrt(power + EPS)
        for r in range(BLOCK // 128):
            some = pl.ds(block * BLOCK + r * 128, 128)
            column = jnp.broadcast_to(factor[r : r + 1], (128, 128)).T
            out[some, :] = (window[some, :] * jnp.concatenate([column] * heads, axis=1)).astype(BF16)
        store = pltpu.make_async_copy(out.at[rows], out_hbm.at[rows], out_sem.at[block])
        store.start()
        stores.append(store)

    swap_out.wait_send()
    for copy in edges:
        copy.wait_send()
    swap_back.wait_send()

    @pl.when(is_owner)
    def _():
        settle(arrived, pieces - 1, send_sem.at[3])
        settle(gathered, chips - 1, send_sem.at[4])

    @pl.when(jnp.logical_not(is_owner))
    def _():
        settle(arrived, pieces, send_sem.at[3])

    for block in range(blocks):
        settle(power_all.at[block], head_n - 1, send_sem.at[6 + block])
    for store in stores:
        store.wait()


def solution(mesh):
    seq_n, head_n = mesh.shape["seq"], mesh.shape["head"]
    z_n = 8

    def local(feat_q, feat_k, values, win_q, win_k, win_v, head_gain):
        tokens, width = values.shape
        heads = head_gain.shape[0]
        first, second, scale_k, scale_q, normal_row = feature_tables(heads)
        chips = seq_n // 2
        pieces = heads // 2 * ROWS // PIECE
        blocks = tokens // BLOCK
        dims = (seq_n, head_n, z_n, heads, tokens, normal_row)
        anywhere = pl.BlockSpec(memory_space=pl.ANY)
        vm = pltpu.VMEM
        return pl.pallas_call(
            functools.partial(mixer, dims),
            out_shape=jax.ShapeDtypeStruct((tokens, width), BF16),
            in_specs=[anywhere] * 6 + [pl.BlockSpec(memory_space=pltpu.SMEM)] + [anywhere] * 4,
            out_specs=anywhere,
            scratch_shapes=[
                vm(feat_q.shape, BF16), vm(feat_k.shape, BF16),
                vm(values.shape, BF16), vm(values.shape, BF16), vm(values.shape, BF16), vm(values.shape, BF16),
                vm((heads, ROWS, 128), BF16), vm((heads, ROWS, 128), BF16), vm((ROWS, 128), F32), vm((8, ROWS), F32),
                vm((W, width), BF16), vm((W, width), BF16),
                vm((heads, ROWS, HD), F32),
                vm((2 * pieces, PIECE, HD), F32),
                vm((pieces, PIECE, HD), F32),
                vm((pieces, PIECE, HD), F32),
                vm((chips, PIECE, HD), F32),
                vm((chips, PIECE, HD), F32),
                vm((pieces, PIECE, HD), F32),
                vm((pieces, PIECE, HD), F32),
                vm((2 * pieces, PIECE, HD), F32),
                vm((heads, tokens, 2 * HD), F32),
                vm((tokens, width), F32),
                vm((heads, tokens, ROWS), BF16),
                vm((blocks, BLOCK // 128, 128), F32),
                vm((blocks, head_n, BLOCK // 128, 128), F32),
                vm((tokens, HD), F32),
                vm((tokens, width), BF16),
                pltpu.SemaphoreType.DMA((10,)),
                pltpu.SemaphoreType.DMA((blocks,)),
                pltpu.SemaphoreType.DMA((6 + blocks,)),
                pltpu.SemaphoreType.DMA((6 + blocks,)),
            ],
            compiler_params=pltpu.CompilerParams(
                collective_id=0, has_side_effects=True, vmem_limit_bytes=48 * 2**20
            ),
            name="mixer",
        )(
            feat_q, feat_k, values, win_q, win_k, win_v, head_gain,
            jnp.asarray(first, BF16), jnp.asarray(second, BF16), jnp.asarray(scale_k), jnp.asarray(scale_q),
        )

    placed = (P("seq", "head"),) * 6 + (P("head"),)
    return jax.shard_map(local, mesh=mesh, in_specs=placed, out_specs=P("seq", "head"), check_vma=False)
```

time: 287 us -> 52.6 us (0.18); the launches traced: 284 us -> 52.3 us
  other arithmetic: 100 us -> 0 us
  waiting for transfers between devices: 65.3 us -> 0 us
  blocking collectives: 60.1 us -> 0 us
  Pallas kernels: 0 us -> 44.3 us
  matrix products: 20.7 us -> 0 us
  between operations: 13.8 us -> 0.08 us
  local copies, waits for them, and re-layouts: 14.8 us -> 7.94 us
  starting transfers between devices: 6.84 us -> 0 us
    select_n x126 -> x0, other arithmetic: 77.9 us -> none  [lap(): jnp.where(position < mine, new, old)]
    all_gather x1 -> x0, waiting for transfers between devices: 65.2 us -> none  [entering(): pieces = jax.tree.map(lambda part: lax.all_gather(part, axis), value)]
    all_gather x1 -> x0, blocking collectives: 51.7 us -> none  [entering(): pieces = jax.tree.map(lambda part: lax.all_gather(part, axis), value)]
    pallas_call x0 -> x1, Pallas kernels: none -> 44.3 us  [local(): pl.pallas_call(functools.partial(mixer, dims), out_shape=jax.ShapeDtypeSt...]
    dot_general x14 -> x0, matrix products: 20.7 us -> none  [the longest x2 5.13 us: local(): jnp.einsum('qhf,hfd->qhd', block_map, run_state, precision=highest_setting)]
    psum x1 -> x0, blocking collectives: 8.42 us -> none  [local(): squares = lax.psum(jnp.sum(combined * combined, axis=1), 'head')]
    ppermute x2 -> x0, starting transfers between devices: 6.83 us -> none  [shifted(): lax.ppermute(value, axis, [(source, source + steps) for source in range(l...]
    slice x6 -> x0, local copies, waits for them, and re-layouts: 6.2 us -> none  [the longest x1 2.25 us: local(): queries[covered_rows]]
  transfers between devices with their start and end apart: 3 -> 0, of which waited for: 1 -> 0; matrix products, arithmetic and copies ran while one was open for 11% -> 0% of each run, Pallas kernels for 0% -> 0%
where the time goes in v1:
time: 52.6 us; the launch traced here: 52.3 us
  Pallas kernels  44.3 us (84%)
  local copies, waits for them, and re-layouts  7.94 us (15%)
    pallas_call x1, Pallas kernels, local(): pl.pallas_call(functools.partial(mixer, dims), out_shape=jax.ShapeDtypeSt...  44.3 us
    unnamed x23, local copies, waits for them, and re-layouts  7.94 us

profile of v1, /device:TPU:1, one launch (start us, length us, event | category | flops | bytes accessed | tf_op | source)
XLA Modules:
  0.0 52.3 jit_solution(6389576594473672464)
XLA Ops:
  0.0 0.0 copy-start.9
  0.0 0.0 copy-start.6
  0.0 1.1 %copy.12.fq_hbm = bf16[1024,64]{1,0:T(8,128)(2,1)S(1)} copy(bf16[1024,64]{0,1:T(8,128)(2,1)} %param.11) | data formatting | bytes 262144 | tf_op args[0]
  1.1 0.0 copy-done.9
  1.1 0.0 copy-start.4
  1.1 0.0 copy-start.5
  1.2 0.0 copy-start.7
  1.2 0.0 copy-start.8
  1.2 0.2 copy.13.fk_hbm
  1.4 0.0 copy-done.6
  1.4 0.7 %copy-done.4 = bf16[4,160,128]{2,1,0:T(8,128)(2,1)S(1)} copy-done((bf16[4,160,128]{2,1,0:T(8,128)(2,1)S(1)}, bf16[4,160,128]{2,1,0:T(8,128)(2,1)}, u32[]{:S(2)}) %copy-start.4) | copy-done | bytes 163864
  2.1 0.1 copy-done.5
  2.1 0.0 copy-done.7
  2.1 0.0 copy-done.8
  2.1 0.0 copy-start
  2.1 1.2 %copy-done = bf16[1024,512]{1,0:T(8,128)(2,1)S(1)} copy-done((bf16[1024,512]{1,0:T(8,128)(2,1)S(1)}, bf16[1024,512]{1,0:T(8,128)(2,1)}, u32[]{:S(2)}) %copy-start) | copy-done | bytes 1048600
  3.4 0.0 copy-start.1
  3.4 1.2 %copy-done.1 = bf16[1024,512]{1,0:T(8,128)(2,1)S(1)} copy-done((bf16[1024,512]{1,0:T(8,128)(2,1)S(1)}, bf16[1024,512]{1,0:T(8,128)(2,1)}, u32[]{:S(2)}) %copy-start.1) | copy-done | bytes 1048600
  4.6 0.0 copy-start.2
  4.6 1.2 %copy-done.2 = bf16[1024,512]{1,0:T(8,128)(2,1)S(1)} copy-done((bf16[1024,512]{1,0:T(8,128)(2,1)S(1)}, bf16[1024,512]{1,0:T(8,128)(2,1)}, u32[]{:S(2)}) %copy-start.2) | copy-done | bytes 1048600
  5.8 0.0 copy-start.3
  5.8 1.2 %copy-done.3 = bf16[1024,512]{1,0:T(8,128)(2,1)S(1)} copy-done((bf16[1024,512]{1,0:T(8,128)(2,1)S(1)}, bf16[1024,512]{1,0:T(8,128)(2,1)}, u32[]{:S(2)}) %copy-start.3) | copy-done | bytes 1048600
  7.0 44.3 %mixer.1 = bf16[1024,512]{1,0:T(8,128)(2,1)S(1)} custom-call(bf16[1024,64]{1,0:T(8,128)(2,1)S(1)} %copy.12.fq_hbm, bf16[1024,64]{1,0:T(8,128)(2,1)S(1)} %copy.13.fk_hbm, bf16[1024,512]{1,0:T(8,128)(2,1)S(1)} %copy-done, bf16[1024,512]{1,0:T(8,128)(2,1)S(1)} %copy-done.1, bf16[1024,512]{1,0:T(8,128)(2,1)S(1)} %copy-done.2, bf16[1024,512]{1,0:T(8,128)(2,1)S(1)} %copy-done.3, ...), custom_call_target="tpu_custom_call" | custom-call | tf_op jit(solution)/shard_map/mixer/pallas_call | solution.py:398
  51.4 1.0 %copy.15 = bf16[1024,512]{1,0:T(8,128)(2,1)} copy(bf16[1024,512]{1,0:T(8,128)(2,1)S(1)} %mixer.1) | data formatting | bytes 2097152
Async XLA Ops:
  0.0 1.1 %copy-start.9 = (bf16[1024,64]{0,1:T(8,128)(2,1)S(1)}, bf16[1024,64]{0,1:T(8,128)(2,1)}, u32[]{:S(2)}) copy-start(bf16[1024,64]{0,1:T(8,128)(2,1)} %param.12) | copy-start | bytes 393220
  0.0 1.4 %copy-start.6 = (f32[160,128]{1,0:T(8,128)S(1)}, f32[160,128]{1,0:T(8,128)}, u32[]{:S(2)}) copy-start(f32[160,128]{1,0:T(8,128)} %constant.10.clone.sk_hbm) | copy-start | bytes 245764
  1.1 0.9 %copy-start.4 = (bf16[4,160,128]{2,1,0:T(8,128)(2,1)S(1)}, bf16[4,160,128]{2,1,0:T(8,128)(2,1)}, u32[]{:S(2)}) copy-start(bf16[4,160,128]{2,1,0:T(8,128)(2,1)} %constant.9.clone.eb_hbm) | copy-start | bytes 491524
  1.1 1.0 %copy-start.5 = (bf16[4,160,128]{2,1,0:T(8,128)(2,1)S(1)}, bf16[4,160,128]{2,1,0:T(8,128)(2,1)}, u32[]{:S(2)}) copy-start(bf16[4,160,128]{2,1,0:T(8,128)(2,1)} %constant.8.clone.ea_hbm) | copy-start | bytes 491524
  1.2 1.0 %copy-start.7 = (f32[8,160]{1,0:T(8,128)S(1)}, f32[8,160]{1,0:T(8,128)}, u32[]{:S(2)}) copy-start(f32[8,160]{1,0:T(8,128)} %constant.11.clone.sq_hbm) | copy-start | bytes 15364
  1.2 1.0 %copy-start.8 = (f32[4]{0:T(128)S(1)}, f32[4]{0:T(128)}, u32[]{:S(2)}) copy-start(f32[4]{0:T(128)} %gain.1) | copy-start | bytes 52
  2.1 1.2 %copy-start = (bf16[1024,512]{1,0:T(8,128)(2,1)S(1)}, bf16[1024,512]{1,0:T(8,128)(2,1)}, u32[]{:S(2)}) copy-start(bf16[1024,512]{1,0:T(8,128)(2,1)} %v_hbm.1) | copy-start | bytes 3145732
  3.4 1.2 %copy-start.1 = (bf16[1024,512]{1,0:T(8,128)(2,1)S(1)}, bf16[1024,512]{1,0:T(8,128)(2,1)}, u32[]{:S(2)}) copy-start(bf16[1024,512]{1,0:T(8,128)(2,1)} %wq_hbm.1) | copy-start | bytes 3145732
  4.6 1.2 %copy-start.2 = (bf16[1024,512]{1,0:T(8,128)(2,1)S(1)}, bf16[1024,512]{1,0:T(8,128)(2,1)}, u32[]{:S(2)}) copy-start(bf16[1024,512]{1,0:T(8,128)(2,1)} %wk_hbm.1) | copy-start | bytes 3145732
  5.8 1.2 %copy-start.3 = (bf16[1024,512]{1,0:T(8,128)(2,1)S(1)}, bf16[1024,512]{1,0:T(8,128)(2,1)}, u32[]{:S(2)}) copy-start(bf16[1024,512]{1,0:T(8,128)(2,1)} %wv_hbm.1) | copy-start | bytes 3145732

commit v2 on v1

v2 whole, which is shorter than its diff:
```python
import functools
import math

import jax
import jax.numpy as jnp
import numpy as np
from jax import lax
from jax.experimental import pallas as pl
from jax.experimental.pallas import tpu as pltpu
from jax.sharding import PartitionSpec as P

MESH = pl.DeviceIdType.MESH
F32 = jnp.float32
BF16 = jnp.bfloat16

W = 64
BLOCK = 512
FEAT = 16
HD = 128
ROWS = 160
PIECE = 10
SLOT = 16
PIECES = ROWS // PIECE
WIDE = PIECES * SLOT
QUAD = 1.0 / (4.0 * math.sqrt(2.0))
EPS = 1e-06


def feature_tables(heads):
    ones_lane = heads * FEAT
    first = np.zeros((heads, ROWS, 128), np.float32)
    second = np.zeros((heads, ROWS, 128), np.float32)
    scale_k = np.zeros((ROWS,), np.float32)
    scale_q = np.zeros((ROWS,), np.float32)
    row = 0
    for shift in range(FEAT // 2 + 1):
        for a in range(FEAT if shift < FEAT // 2 else FEAT // 2):
            for h in range(heads):
                first[h, row, h * FEAT + a] = 1.0
                second[h, row, h * FEAT + (a + shift) % FEAT] = 1.0
            scale_k[row] = QUAD
            scale_q[row] = np.float32(QUAD) * (1.0 if shift == 0 else 2.0)
            row += 1
    for a in range(FEAT):
        for h in range(heads):
            first[h, row, h * FEAT + a] = 1.0
            second[h, row, ones_lane] = 1.0
        scale_k[row] = scale_q[row] = 0.5
        row += 1
    first[:, row, ones_lane] = 1.0
    second[:, row, ones_lane] = 1.0
    scale_k[row] = scale_q[row] = 1.0
    row += 1
    assert row + 2 <= ROWS
    spot = np.arange(ROWS) // PIECE * SLOT + np.arange(ROWS) % PIECE
    first_q = np.zeros((heads, WIDE, 128), np.float32)
    second_q = np.zeros((heads, WIDE, 128), np.float32)
    first_q[:, spot], second_q[:, spot] = first, second
    wide_k = np.ascontiguousarray(np.broadcast_to(scale_k[:, None], (ROWS, 128)))
    wide_q = np.zeros((8, WIDE), np.float32)
    wide_q[:, spot] = scale_q
    return first, second, first_q, second_q, wide_k, wide_q, row


def dot(a, b):
    return jnp.dot(a, b, preferred_element_type=F32)


def dot_nt(a, b):
    return lax.dot_general(a, b, (((1,), (1,)), ((), ())), preferred_element_type=F32)


def split(x):
    high = x.astype(BF16)
    return high, (x - high.astype(F32)).astype(BF16)


def mixer(
    dims,
    fq_hbm, fk_hbm, v_hbm, wq_hbm, wk_hbm, wv_hbm, gain, ea_hbm, eb_hbm, eaq_hbm, ebq_hbm, sk_hbm, sq_hbm,
    out,
    fq, fk, v, wq, wk, wv, ea, eb, eaq, ebq, sk, sq,
    edge_k, edge_v, first_state, total, got, chip_sum, gathered, prefixes, arrived, payload, before,
    fq_rows, local, window, map_q, power_own, power_all, squares,
    in_sem, send_sem, recv_sem,
):
    seq_n, head_n, z_n, heads, tokens, normal_row = dims
    x_n = seq_n // 2 // z_n
    chips = seq_n // 2
    half = heads // 2
    pieces = half * PIECES
    blocks = tokens // BLOCK
    me, head = lax.axis_index("seq"), lax.axis_index("head")
    core = lax.rem(me, 2)
    chip = me // 2
    other = me + 1 - 2 * core

    def load(index, src, dst):
        return pltpu.make_async_copy(src, dst, in_sem.at[index])

    loads = [
        load(0, fk_hbm, fk.at[pl.ds(0, heads * FEAT)]),
        load(1, ea_hbm, ea), load(2, eb_hbm, eb), load(3, sk_hbm, sk),
        load(4, v_hbm, v), load(5, fq_hbm, fq.at[pl.ds(0, heads * FEAT)]), load(6, sq_hbm, sq),
        load(10, eaq_hbm, eaq), load(11, ebq_hbm, ebq), load(7, wk_hbm, wk), load(8, wq_hbm, wq), load(9, wv_hbm, wv),
    ]
    for copy in loads:
        copy.start()

    def remote(src, dst, index, seq, group):
        return pltpu.make_async_remote_copy(
            src_ref=src, dst_ref=dst, send_sem=send_sem.at[index], recv_sem=recv_sem.at[index],
            device_id=(seq, group), device_id_type=MESH,
        )

    def settle(buffer, count, sem, rows=PIECE):
        part = buffer.at[pl.ds(0, count), pl.ds(0, rows)]
        pltpu.make_async_copy(part, part, sem).wait()

    barrier = pltpu.get_barrier_semaphore()
    edge_mate = lax.rem(me + 2 * core - 1 + seq_n, seq_n)

    def greet(seq, group):
        pl.semaphore_signal(barrier, inc=1, device_id=(seq, group), device_id_type=MESH)

    greet(other, head)
    greet(edge_mate, head)
    for step in range(1, head_n):
        greet(me, lax.rem(head + step, head_n))

    def greet_chip(step, carry):
        greet(2 * lax.rem(chip + step, chips) + core, head)
        return carry

    lax.fori_loop(1, chips, greet_chip, 0)
    for ref in (first_state, total, arrived):
        ref[...] = jnp.zeros_like(ref)

    lanes = lax.broadcasted_iota(jnp.int32, (128, 128), 1)
    subs = lax.broadcasted_iota(jnp.int32, (128, 128), 0)
    eye = lanes == subs
    row_ids = lax.broadcasted_iota(jnp.int32, (ROWS, HD), 0)
    spots = row_ids + row_ids // PIECE * (SLOT - PIECE) - lax.broadcasted_iota(jnp.int32, (ROWS, HD), 1)
    ones_v = jnp.ones((BLOCK, HD), BF16)
    feats = heads * FEAT
    tail = jnp.where(lax.broadcasted_iota(jnp.int32, (128 - feats, tokens), 0) == 0, 1.0, 0.0).astype(BF16)
    fk[pl.ds(feats, 128 - feats), :] = tail
    fq[pl.ds(feats, 128 - feats), :] = tail
    for index in range(4):
        loads[index].wait()
    loads[4].wait()

    def put(ref, h, state):
        for piece in range(PIECES):
            ref[h * PIECES + piece, 0:PIECE, :] = state[piece * PIECE : (piece + 1) * PIECE]

    def state_of(h):
        cols = pl.ds(pl.multiple_of(h * HD, HD), HD)
        summed = None
        for block in range(blocks):
            keys = fk[:, pl.ds(block * BLOCK, BLOCK)]
            scale = sk[...]
            mapped = dot(ea[h], keys) * dot(eb[h], keys)
            mapped = (mapped * jnp.concatenate([scale] * (BLOCK // 128), axis=1)).astype(BF16)
            both = dot(mapped, jnp.concatenate([v[pl.ds(block * BLOCK, BLOCK), cols], ones_v], axis=1))
            state, normal = both[:, :HD], both[:, HD:]
            low = jnp.sum(jnp.where(spots == 0, normal, 0.0), axis=0, keepdims=True)
            high = jnp.sum(jnp.where(spots == HD, normal, 0.0), axis=0, keepdims=True)
            state = jnp.where(row_ids == normal_row, low, jnp.where(row_ids == normal_row + 1, high, state))
            if block == 0:
                put(first_state, h, state)
            summed = state if summed is None else summed + state
        put(total, h, summed)

    def states(start):
        def body(i, carry):
            state_of(start + i)
            return carry
        lax.fori_loop(0, half, body, 0, unroll=True)

    states(half * (1 - core))
    pl.semaphore_wait(barrier, 1 + 1 + head_n - 1 + chips - 1)
    swap_out = remote(total.at[pl.ds((1 - core) * pieces, pieces)], got, 0, other, head)
    swap_out.start()
    states(half * core)

    following = lax.rem(me + 1, seq_n)
    edges = [
        remote(wk_hbm.at[pl.ds(tokens - W, W)], edge_k, 1, following, head),
        remote(wv_hbm.at[pl.ds(tokens - W, W)], edge_v, 2, following, head),
    ]
    for copy in edges:
        copy.start()
    swap_out.wait_recv()
    own = pl.ds(core * pieces, pieces)
    chip_sum[...] = total[own] + got[...]

    def far_first(step):
        away = step // x_n
        along_z = lax.rem(z_n // 2 + jnp.where(lax.rem(away, 2) == 0, away // 2, z_n - (away + 1) // 2), z_n)
        x, z = chip // z_n, lax.rem(chip, z_n)
        return lax.rem(x + lax.rem(step, x_n), x_n) * z_n + lax.rem(z + along_z, z_n)

    def to_chips(src, dst, index):
        def send(step, carry):
            there = far_first(step)

            @pl.when(there != chip)
            def _():
                remote(
                    src.at[there, pl.ds(0, PIECE)], dst.at[chip, pl.ds(0, PIECE)], index, 2 * there + core, head
                ).start()
            return carry

        lax.fori_loop(0, chips, send, 0)
        dst[chip] = src[chip]

    to_chips(chip_sum, gathered, 3)

    for copy in loads[5:]:
        copy.wait()
    quarter = BLOCK // 2
    tri = lax.broadcasted_iota(jnp.int32, (quarter, quarter), 0) >= lax.broadcasted_iota(jnp.int32, (quarter, quarter), 1)
    feat_lane = lax.broadcasted_iota(jnp.int32, (1, 128), 1)
    fq_rows[...] = fq[...].T

    def within(i, carry):
        h, block = i // blocks, lax.rem(i, blocks)
        cols = pl.ds(pl.multiple_of(h * HD, HD), HD)
        start = pl.multiple_of(block * BLOCK, BLOCK)
        keys = fk[:, pl.ds(start, BLOCK)]
        mine = jnp.where(feat_lane // FEAT == h, 1.0, 0.0).astype(BF16)
        ext = fq_rows[pl.ds(start, BLOCK), :]
        queries = ext * mine
        vals = jnp.concatenate([v[pl.ds(start, BLOCK), cols], ones_v], axis=1)

        def weights(q, k):
            s = dot(q, k)
            return 1.0 + s * 0.25 + s * s * (1.0 / 32.0)

        top = jnp.where(tri, weights(queries[:quarter], keys[:, :quarter]), 0.0).astype(BF16)
        local[h, pl.ds(start, quarter), :] = dot(top, vals[:quarter])
        left = weights(queries[quarter:], keys[:, :quarter]).astype(BF16)
        right = jnp.where(tri, weights(queries[quarter:], keys[:, quarter:]), 0.0).astype(BF16)
        local[h, pl.ds(start + quarter, quarter), :] = dot(jnp.concatenate([left, right], axis=1), vals)
        mapped = dot_nt(ext, eaq[h]) * dot_nt(ext, ebq[h]) * sq[0:1, :]
        map_q[h, pl.ds(start, BLOCK), :] = mapped.astype(BF16)
        return carry

    lax.fori_loop(0, heads * blocks, within, 0, unroll=4)

    settle(gathered, chips - 1, recv_sem.at[3])

    def add(u, run):
        prefixes[u] = run
        return run + gathered[u]

    lax.fori_loop(0, chips, add, jnp.zeros((SLOT, HD), F32), unroll=8)
    to_chips(prefixes, arrived, 4)

    band_row = lax.broadcasted_iota(jnp.int32, (W, 2 * W), 0)
    band_col = lax.broadcasted_iota(jnp.int32, (W, 2 * W), 1)
    band = (band_col > band_row) & (band_col <= band_row + W)
    sharp = 1.0 / math.sqrt(HD)

    def attend(scores, allowed):
        scores = jnp.where(allowed, scores * sharp, -1e30)
        weights = jnp.exp(scores - jnp.max(scores, axis=1, keepdims=True))
        return (weights / jnp.sum(weights, axis=1, keepdims=True)).astype(BF16)

    group = 8
    band_group = jnp.concatenate([band] * group, axis=0)

    def windows(h, first, count):
        cols = pl.ds(pl.multiple_of(h * HD, HD), HD)
        starts = [first + c * W for c in range(count)]
        scores = [
            dot_nt(wq[pl.ds(s, W), cols], wk[pl.ds(s - W, 2 * W), cols]) for s in starts
        ]
        probs = attend(jnp.concatenate(scores, axis=0), band_group[: count * W])
        for c, s in enumerate(starts):
            window[pl.ds(s, W), cols] = dot(probs[c * W : (c + 1) * W], wv[pl.ds(s - W, 2 * W), cols])

    def window_head(h, carry):
        windows(h, W, group - 1)

        def rest(g, inner):
            windows(h, pl.multiple_of(g * group * W, group * W), group)
            return inner

        return lax.fori_loop(1, tokens // (group * W), rest, carry, unroll=True)

    lax.fori_loop(0, heads, window_head, 0)

    edges[0].wait_recv()
    edges[1].wait_recv()
    band_first = band & ((band_col >= W) | (me > 0))

    def window_edge(h, carry):
        cols = pl.ds(pl.multiple_of(h * HD, HD), HD)
        keys = jnp.concatenate([edge_k[:, cols], wk[pl.ds(0, W), cols]], axis=0)
        vals = jnp.concatenate([edge_v[:, cols], wv[pl.ds(0, W), cols]], axis=0)
        probs = attend(dot_nt(wq[pl.ds(0, W), cols], keys), band_first)
        window[pl.ds(0, W), cols] = dot(probs, vals)
        return carry

    lax.fori_loop(0, heads, window_edge, 0, unroll=True)

    settle(arrived, chips - 1, recv_sem.at[4])
    ahead = jnp.where(core == 0, 1.0, 0.0)
    payload[...] = arrived[...] + total[own] * ahead
    swap_back = remote(payload, before.at[own], 5, other, head)
    swap_back.start()
    before[own] = arrived[...] + got[...] * (1.0 - ahead)

    spot = normal_row // PIECE * SLOT + normal_row % PIECE

    def finish(h, block, fresh):
        cols = pl.ds(pl.multiple_of(h * HD, HD), HD)
        rows = pl.ds(block * BLOCK, BLOCK)
        mine = pl.ds(h * PIECES, PIECES)
        state = before[mine]
        if block > 0:
            state = state + first_state[mine]
        state = state.reshape(WIDE, HD)
        normal = jnp.concatenate(
            [jnp.broadcast_to(state[spot + i : spot + i + 1], (HD, HD)).T for i in range(2)], axis=0
        )
        high, low = split(jnp.concatenate([state, normal], axis=1))
        mapped = map_q[h, rows, :]
        sums = dot(mapped, high) + dot(mapped, low) + local[h, rows, :]
        combined = gain[h] * (sums[:, :HD] / sums[:, HD:] + window[rows, cols])
        window[rows, cols] = combined
        squared = combined * combined
        squares[rows, :] = squared if fresh else squares[rows, :] + squared

    own_head = half * core
    for block in range(blocks):
        finish(own_head, block, True)
    for i in range(1, half):
        for block in range(blocks):
            finish(own_head + i, block, False)
    swap_back.wait_recv()
    for block in range(blocks):
        for i in range(half):
            finish(half * (1 - core) + i, block, False)
        sums = jnp.sum(squares[pl.ds(block * BLOCK, BLOCK), :], axis=1, keepdims=True)
        for r in range(BLOCK // 128):
            wide = jnp.broadcast_to(sums[r * 128 : (r + 1) * 128], (128, 128))
            power_own[block, r : r + 1, :] = jnp.sum(jnp.where(eye, wide, 0.0), axis=0, keepdims=True)
        power_all[block, head] = power_own[block]
        for step in range(1, head_n):
            remote(
                power_own.at[block], power_all.at[block, head], 6 + block, me, lax.rem(head + step, head_n)
            ).start()

    for block in range(blocks):
        settle(power_all.at[block], head_n - 1, recv_sem.at[6 + block], BLOCK // 128)
        power = jnp.sum(power_all[block], axis=0) * (1.0 / (heads * head_n * HD))
        factor = lax.rsqrt(power + EPS)
        for r in range(BLOCK // 128):
            some = pl.ds(block * BLOCK + r * 128, 128)
            column = jnp.broadcast_to(factor[r : r + 1], (128, 128)).T
            out[some, :] = (window[some, :] * jnp.concatenate([column] * heads, axis=1)).astype(BF16)

    swap_out.wait_send()
    for copy in edges:
        copy.wait_send()
    swap_back.wait_send()

    settle(gathered, chips - 1, send_sem.at[3])
    settle(arrived, chips - 1, send_sem.at[4])
    for block in range(blocks):
        settle(power_all.at[block], head_n - 1, send_sem.at[6 + block], BLOCK // 128)


def solution(mesh):
    seq_n, head_n = mesh.shape["seq"], mesh.shape["head"]
    z_n = 8

    def local(feat_q, feat_k, values, win_q, win_k, win_v, head_gain):
        tokens, width = values.shape
        heads = head_gain.shape[0]
        *tables, normal_row = feature_tables(heads)
        chips = seq_n // 2
        pieces = heads // 2 * PIECES
        blocks = tokens // BLOCK
        dims = (seq_n, head_n, z_n, heads, tokens, normal_row)
        anywhere = pl.BlockSpec(memory_space=pltpu.HBM)
        vm = pltpu.VMEM
        stay = functools.partial(pltpu.with_memory_space_constraint, memory_space=pltpu.HBM)
        return pl.pallas_call(
            functools.partial(mixer, dims),
            out_shape=jax.ShapeDtypeStruct((tokens, width), BF16),
            in_specs=[anywhere] * 6 + [pl.BlockSpec(memory_space=pltpu.SMEM)] + [anywhere] * 6,
            out_specs=pl.BlockSpec(memory_space=pltpu.VMEM),
            scratch_shapes=[
                vm((128, tokens), BF16), vm((128, tokens), BF16),
                vm(values.shape, BF16), vm(values.shape, BF16), vm(values.shape, BF16), vm(values.shape, BF16),
                vm((heads, ROWS, 128), BF16), vm((heads, ROWS, 128), BF16),
                vm((heads, WIDE, 128), BF16), vm((heads, WIDE, 128), BF16), vm((ROWS, 128), F32), vm((8, WIDE), F32),
                vm((W, width), BF16), vm((W, width), BF16),
                vm((2 * pieces, SLOT, HD), F32),
                vm((2 * pieces, SLOT, HD), F32),
                vm((pieces, SLOT, HD), F32),
                vm((pieces, SLOT, HD), F32),
                vm((chips, SLOT, HD), F32),
                vm((chips, SLOT, HD), F32),
                vm((pieces, SLOT, HD), F32),
                vm((pieces, SLOT, HD), F32),
                vm((2 * pieces, SLOT, HD), F32),
                vm((tokens, 128), BF16),
                vm((heads, tokens, 2 * HD), F32),
                vm((tokens, width), F32),
                vm((heads, tokens, WIDE), BF16),
                vm((blocks, BLOCK // 128, 128), F32),
                vm((blocks, head_n, BLOCK // 128, 128), F32),
                vm((tokens, HD), F32),
                pltpu.SemaphoreType.DMA((12,)),
                pltpu.SemaphoreType.DMA((6 + blocks,)),
                pltpu.SemaphoreType.DMA((6 + blocks,)),
            ],
            compiler_params=pltpu.CompilerParams(
                collective_id=0, has_side_effects=True, vmem_limit_bytes=48 * 2**20
            ),
            name="mixer",
        )(
            *(stay(x) for x in (feat_q.T, feat_k.T, values, win_q, win_k, win_v, head_gain)),
            *(stay(x) for x in (
                *(jnp.asarray(table, BF16) for table in tables[:4]), *(jnp.asarray(table) for table in tables[4:]),
            )),
        )

    placed = (P("seq", "head"),) * 6 + (P("head"),)
    return jax.shard_map(local, mesh=mesh, in_specs=placed, out_specs=P("seq", "head"), check_vma=False)
```

time: 52.6 us -> 36.6 us (0.70)
  Pallas kernels: 44.3 us -> 35.6 us
  local copies, waits for them, and re-layouts: 7.94 us -> 0.97 us
    pallas_call x1, Pallas kernels: 44.3 us -> 35.6 us  [local(): pl.pallas_call(functools.partial(mixer, dims), out_shape=jax.ShapeDtypeSt...]
    unnamed x23 -> x1, local copies, waits for them, and re-layouts: 7.94 us -> 0.97 us
where the time goes in v2:
time: 36.6 us
  Pallas kernels  35.6 us (97%)
  local copies, waits for them, and re-layouts  0.97 us (3%)
    pallas_call x1, Pallas kernels, local(): pl.pallas_call(functools.partial(mixer, dims), out_shape=jax.ShapeDtypeSt...  35.6 us
    unnamed x1, local copies, waits for them, and re-layouts  0.97 us

profile of v2, /device:TPU:1, one launch (start us, length us, event | category | flops | bytes accessed | tf_op | source)
XLA Modules:
  0.0 36.6 jit_solution(18033174587403562118)
XLA Ops:
  0.0 35.6 %mixer.1 = bf16[1024,512]{1,0:T(8,128)(2,1)S(1)} custom-call(bf16[64,1024]{1,0:T(8,128)(2,1)} %bitcast.2, bf16[64,1024]{1,0:T(8,128)(2,1)} %bitcast.3, bf16[1024,512]{1,0:T(8,128)(2,1)} %v_hbm.1, bf16[1024,512]{1,0:T(8,128)(2,1)} %wq_hbm.1, bf16[1024,512]{1,0:T(8,128)(2,1)} %wk_hbm.1, bf16[1024,512]{1,0:T(8,128)(2,1)} %wv_hbm.1, f32[4]{0:T(128)} %gain.1, ...), custom_call_target="tpu_custom_call" | custom-call | tf_op jit(solution)/shard_map/mixer/pallas_call | solution.py:392
  35.6 1.0 %copy.15 = bf16[1024,512]{1,0:T(8,128)(2,1)} copy(bf16[1024,512]{1,0:T(8,128)(2,1)S(1)} %mixer.1) | data formatting | bytes 2097152

commit v3 on v2

--- a/solution.py
+++ b/solution.py
@@ -98,14 +98,12 @@
     def load(index, src, dst):
         return pltpu.make_async_copy(src, dst, in_sem.at[index])
 
-    loads = [
-        load(0, fk_hbm, fk.at[pl.ds(0, heads * FEAT)]),
-        load(1, ea_hbm, ea), load(2, eb_hbm, eb), load(3, sk_hbm, sk),
-        load(4, v_hbm, v), load(5, fq_hbm, fq.at[pl.ds(0, heads * FEAT)]), load(6, sq_hbm, sq),
-        load(10, eaq_hbm, eaq), load(11, ebq_hbm, ebq), load(7, wk_hbm, wk), load(8, wq_hbm, wq), load(9, wv_hbm, wv),
+    first_loads = [load(0, fk_hbm, fk.at[pl.ds(0, heads * FEAT)]), load(1, ea_hbm, ea), load(2, eb_hbm, eb), load(3, sk_hbm, sk)]
+    first_loads.append(load(4, v_hbm, v))
+    later_loads = [
+        load(5, fq_hbm, fq.at[pl.ds(0, heads * FEAT)]), load(6, sq_hbm, sq), load(10, eaq_hbm, eaq), load(11, ebq_hbm, ebq),
+        load(7, wk_hbm, wk), load(8, wq_hbm, wq), load(9, wv_hbm, wv),
     ]
-    for copy in loads:
-        copy.start()
 
     def remote(src, dst, index, seq, group):
         return pltpu.make_async_remote_copy(
@@ -123,16 +121,20 @@
     def greet(seq, group):
         pl.semaphore_signal(barrier, inc=1, device_id=(seq, group), device_id_type=MESH)
 
+    x, z = chip // z_n, lax.rem(chip, z_n)
+    away = sorted(
+        ((dx, dz) for dx in range(x_n) for dz in range(z_n) if dx or dz),
+        key=lambda d: -(min(d[0], x_n - d[0]) + 1.01 * min(d[1], z_n - d[1])),
+    )
+    others = [lax.rem(x + dx, x_n) * z_n + lax.rem(z + dz, z_n) for dx, dz in away]
+    for there in others:
+        greet(2 * there + core, head)
     greet(other, head)
     greet(edge_mate, head)
     for step in range(1, head_n):
         greet(me, lax.rem(head + step, head_n))
-
-    def greet_chip(step, carry):
-        greet(2 * lax.rem(chip + step, chips) + core, head)
-        return carry
-
-    lax.fori_loop(1, chips, greet_chip, 0)
+    for copy in first_loads:
+        copy.start()
     for ref in (first_state, total, arrived):
         ref[...] = jnp.zeros_like(ref)
 
@@ -146,9 +148,10 @@
     tail = jnp.where(lax.broadcasted_iota(jnp.int32, (128 - feats, tokens), 0) == 0, 1.0, 0.0).astype(BF16)
     fk[pl.ds(feats, 128 - feats), :] = tail
     fq[pl.ds(feats, 128 - feats), :] = tail
-    for index in range(4):
-        loads[index].wait()
-    loads[4].wait()
+    for copy in first_loads:
+        copy.wait()
+    for copy in later_loads:
+        copy.start()
 
     def put(ref, h, state):
         for piece in range(PIECES):
@@ -195,29 +198,14 @@
     own = pl.ds(core * pieces, pieces)
     chip_sum[...] = total[own] + got[...]
 
-    def far_first(step):
-        away = step // x_n
-        along_z = lax.rem(z_n // 2 + jnp.where(lax.rem(away, 2) == 0, away // 2, z_n - (away + 1) // 2), z_n)
-        x, z = chip // z_n, lax.rem(chip, z_n)
-        return lax.rem(x + lax.rem(step, x_n), x_n) * z_n + lax.rem(z + along_z, z_n)
-
     def to_chips(src, dst, index):
-        def send(step, carry):
-            there = far_first(step)
-
-            @pl.when(there != chip)
-            def _():
-                remote(
-                    src.at[there, pl.ds(0, PIECE)], dst.at[chip, pl.ds(0, PIECE)], index, 2 * there + core, head
-                ).start()
-            return carry
-
-        lax.fori_loop(0, chips, send, 0)
+        for there in others:
+            remote(src.at[there, pl.ds(0, PIECE)], dst.at[chip, pl.ds(0, PIECE)], index, 2 * there + core, head).start()
         dst[chip] = src[chip]
 
     to_chips(chip_sum, gathered, 3)
 
-    for copy in loads[5:]:
+    for copy in later_loads:
         copy.wait()
     quarter = BLOCK // 2
     tri = lax.broadcasted_iota(jnp.int32, (quarter, quarter), 0) >= lax.broadcasted_iota(jnp.int32, (quarter, quarter), 1)
@@ -249,14 +237,24 @@
 
     lax.fori_loop(0, heads * blocks, within, 0, unroll=4)
 
-    settle(gathered, chips - 1, recv_sem.at[3])
-
-    def add(u, run):
-        prefixes[u] = run
-        return run + gathered[u]
-
-    lax.fori_loop(0, chips, add, jnp.zeros((SLOT, HD), F32), unroll=8)
-    to_chips(prefixes, arrived, 4)
+    spot = normal_row // PIECE * SLOT + normal_row % PIECE
+
+    def state_halves(ref, h):
+        state = ref[pl.ds(h * PIECES, PIECES)].reshape(WIDE, HD)
+        normal = jnp.concatenate(
+            [jnp.broadcast_to(state[spot + i : spot + i + 1], (HD, HD)).T for i in range(2)], axis=0
+        )
+        return split(jnp.concatenate([state, normal], axis=1))
+
+    def apply_state(mapped, halves):
+        return dot(mapped, halves[0]) + dot(mapped, halves[1])
+
+    def first_block(h, carry):
+        rows = pl.ds(BLOCK, BLOCK)
+        local[h, rows, :] += apply_state(map_q[h, rows, :], state_halves(first_state, h))
+        return carry
+
+    lax.fori_loop(0, heads, first_block, 0, unroll=2)
 
     band_row = lax.broadcasted_iota(jnp.int32, (W, 2 * W), 0)
     band_col = lax.broadcasted_iota(jnp.int32, (W, 2 * W), 1)
@@ -290,7 +288,18 @@
 
         return lax.fori_loop(1, tokens // (group * W), rest, carry, unroll=True)
 
-    lax.fori_loop(0, heads, window_head, 0)
+    lax.fori_loop(0, half, window_head, 0)
+
+    settle(gathered, chips - 1, recv_sem.at[3])
+
+    def add(u, run):
+        prefixes[u] = run
+        return run + gathered[u]
+
+    lax.fori_loop(0, chips, add, jnp.zeros((SLOT, HD), F32), unroll=8)
+    to_chips(prefixes, arrived, 4)
+
+    lax.fori_loop(half, heads, window_head, 0)
 
     edges[0].wait_recv()
     edges[1].wait_recv()
@@ -306,44 +315,42 @@
 
     lax.fori_loop(0, heads, window_edge, 0, unroll=True)
 
-    settle(arrived, chips - 1, recv_sem.at[4])
     ahead = jnp.where(core == 0, 1.0, 0.0)
-    payload[...] = arrived[...] + total[own] * ahead
-    swap_back = remote(payload, before.at[own], 5, other, head)
+
+    @pl.when(chip > 0)
+    def _():
+        settle(arrived, chips - 1, recv_sem.at[4])
+        payload[...] = arrived[...] + total[own] * ahead
+        before[own] = arrived[...] + got[...] * (1.0 - ahead)
+
+    @pl.when(chip == 0)
+    def _():
+        payload[...] = total[own] * ahead
+        before[own] = got[...] * (1.0 - ahead)
+
+    swap_back = remote(payload, before.at[pl.ds(core * pieces, pieces)], 5, other, head)
     swap_back.start()
-    before[own] = arrived[...] + got[...] * (1.0 - ahead)
-
-    spot = normal_row // PIECE * SLOT + normal_row % PIECE
-
-    def finish(h, block, fresh):
+
+    def finish(h, block, halves, fresh):
         cols = pl.ds(pl.multiple_of(h * HD, HD), HD)
         rows = pl.ds(block * BLOCK, BLOCK)
-        mine = pl.ds(h * PIECES, PIECES)
-        state = before[mine]
-        if block > 0:
-            state = state + first_state[mine]
-        state = state.reshape(WIDE, HD)
-        normal = jnp.concatenate(
-            [jnp.broadcast_to(state[spot + i : spot + i + 1], (HD, HD)).T for i in range(2)], axis=0
-        )
-        high, low = split(jnp.concatenate([state, normal], axis=1))
-        mapped = map_q[h, rows, :]
-        sums = dot(mapped, high) + dot(mapped, low) + local[h, rows, :]
+        sums = apply_state(map_q[h, rows, :], halves) + local[h, rows, :]
         combined = gain[h] * (sums[:, :HD] / sums[:, HD:] + window[rows, cols])
         window[rows, cols] = combined
         squared = combined * combined
         squares[rows, :] = squared if fresh else squares[rows, :] + squared
 
-    own_head = half * core
+    for i in range(half):
+        h = half * core + i
+        halves = state_halves(before, h)
+        for block in range(blocks):
+            finish(h, block, halves, i == 0)
+    swap_back.wait_recv()
+    rest = [half * (1 - core) + i for i in range(half)]
+    rest_halves = [state_halves(before, h) for h in rest]
     for block in range(blocks):
-        finish(own_head, block, True)
-    for i in range(1, half):
-        for block in range(blocks):
-            finish(own_head + i, block, False)
-    swap_back.wait_recv()
-    for block in range(blocks):
-        for i in range(half):
-            finish(half * (1 - core) + i, block, False)
+        for h, halves in zip(rest, rest_halves):
+            finish(h, block, halves, False)
         sums = jnp.sum(squares[pl.ds(block * BLOCK, BLOCK), :], axis=1, keepdims=True)
         for r in range(BLOCK // 128):
             wide = jnp.broadcast_to(sums[r * 128 : (r + 1) * 128], (128, 128))
@@ -362,6 +369,10 @@
             some = pl.ds(block * BLOCK + r * 128, 128)
             column = jnp.broadcast_to(factor[r : r + 1], (128, 128)).T
             out[some, :] = (window[some, :] * jnp.concatenate([column] * heads, axis=1)).astype(BF16)
+
+    @pl.when(chip == 0)
+    def _():
+        settle(arrived, chips - 1, recv_sem.at[4])
 
     swap_out.wait_send()
     for copy in edges:

time: 36.6 us -> 33.8 us (0.923)
  the two profiles are of different devices: /device:TPU:1 before, /device:TPU:3 now
where the time goes in v3:
time: 33.8 us; the launch traced here: 33.6 us
  Pallas kernels  32.7 us (97%)
  local copies, waits for them, and re-layouts  0.97 us (3%)
    pallas_call x1, Pallas kernels, local(): pl.pallas_call(functools.partial(mixer, dims), out_shape=jax.ShapeDtypeSt...  32.7 us
    unnamed x1, local copies, waits for them, and re-layouts  0.97 us

profile of v3, /device:TPU:3, one launch (start us, length us, event | category | flops | bytes accessed | tf_op | source)
XLA Modules:
  0.0 33.6 jit_solution(9288392719421693256)
XLA Ops:
  0.0 32.7 %mixer.1 = bf16[1024,512]{1,0:T(8,128)(2,1)S(1)} custom-call(bf16[64,1024]{1,0:T(8,128)(2,1)} %bitcast.2, bf16[64,1024]{1,0:T(8,128)(2,1)} %bitcast.3, bf16[1024,512]{1,0:T(8,128)(2,1)} %v_hbm.1, bf16[1024,512]{1,0:T(8,128)(2,1)} %wq_hbm.1, bf16[1024,512]{1,0:T(8,128)(2,1)} %wk_hbm.1, bf16[1024,512]{1,0:T(8,128)(2,1)} %wv_hbm.1, f32[4]{0:T(128)} %gain.1, ...), custom_call_target="tpu_custom_call" | custom-call | tf_op jit(solution)/shard_map/mixer/pallas_call | solution.py:403
  32.7 1.0 %copy.15 = bf16[1024,512]{1,0:T(8,128)(2,1)} copy(bf16[1024,512]{1,0:T(8,128)(2,1)S(1)} %mixer.1) | data formatting | bytes 2097152

commit v4 on v3

--- a/solution.py
+++ b/solution.py
@@ -121,6 +121,10 @@
     def greet(seq, group):
         pl.semaphore_signal(barrier, inc=1, device_id=(seq, group), device_id_type=MESH)
 
+    for copy in first_loads:
+        copy.start()
+    for ref in (got, before, arrived):
+        ref[...] = jnp.zeros_like(ref)
     x, z = chip // z_n, lax.rem(chip, z_n)
     away = sorted(
         ((dx, dz) for dx in range(x_n) for dz in range(z_n) if dx or dz),
@@ -133,14 +137,9 @@
     greet(edge_mate, head)
     for step in range(1, head_n):
         greet(me, lax.rem(head + step, head_n))
-    for copy in first_loads:
-        copy.start()
-    for ref in (first_state, total, arrived):
+    for ref in (first_state, total):
         ref[...] = jnp.zeros_like(ref)
 
-    lanes = lax.broadcasted_iota(jnp.int32, (128, 128), 1)
-    subs = lax.broadcasted_iota(jnp.int32, (128, 128), 0)
-    eye = lanes == subs
     row_ids = lax.broadcasted_iota(jnp.int32, (ROWS, HD), 0)
     spots = row_ids + row_ids // PIECE * (SLOT - PIECE) - lax.broadcasted_iota(jnp.int32, (ROWS, HD), 1)
     ones_v = jnp.ones((BLOCK, HD), BF16)
@@ -183,7 +182,7 @@
 
     states(half * (1 - core))
     pl.semaphore_wait(barrier, 1 + 1 + head_n - 1 + chips - 1)
-    swap_out = remote(total.at[pl.ds((1 - core) * pieces, pieces)], got, 0, other, head)
+    swap_out = remote(total.at[pl.ds((1 - core) * pieces, pieces), pl.ds(0, PIECE)], got.at[:, pl.ds(0, PIECE)], 0, other, head)
     swap_out.start()
     states(half * core)
 
@@ -242,12 +241,13 @@
     def state_halves(ref, h):
         state = ref[pl.ds(h * PIECES, PIECES)].reshape(WIDE, HD)
         normal = jnp.concatenate(
-            [jnp.broadcast_to(state[spot + i : spot + i + 1], (HD, HD)).T for i in range(2)], axis=0
+            [jnp.broadcast_to(state[spot + i : spot + i + 1], (HD, HD)) for i in range(2)], axis=1
         )
-        return split(jnp.concatenate([state, normal], axis=1))
+        return jnp.concatenate(split(state), axis=1), jnp.concatenate(split(normal), axis=0)
 
     def apply_state(mapped, halves):
-        return dot(mapped, halves[0]) + dot(mapped, halves[1])
+        upper, lower = dot(mapped, halves[0]), dot_nt(mapped, halves[1])
+        return jnp.concatenate([upper[:, :HD] + upper[:, HD:], lower[:, :HD] + lower[:, HD:]], axis=1)
 
     def first_block(h, carry):
         rows = pl.ds(BLOCK, BLOCK)
@@ -288,8 +288,6 @@
 
         return lax.fori_loop(1, tokens // (group * W), rest, carry, unroll=True)
 
-    lax.fori_loop(0, half, window_head, 0)
-
     settle(gathered, chips - 1, recv_sem.at[3])
 
     def add(u, run):
@@ -299,7 +297,7 @@
     lax.fori_loop(0, chips, add, jnp.zeros((SLOT, HD), F32), unroll=8)
     to_chips(prefixes, arrived, 4)
 
-    lax.fori_loop(half, heads, window_head, 0)
+    lax.fori_loop(0, heads, window_head, 0)
 
     edges[0].wait_recv()
     edges[1].wait_recv()
@@ -328,7 +326,7 @@
         payload[...] = total[own] * ahead
         before[own] = got[...] * (1.0 - ahead)
 
-    swap_back = remote(payload, before.at[pl.ds(core * pieces, pieces)], 5, other, head)
+    swap_back = remote(payload.at[:, pl.ds(0, PIECE)], before.at[pl.ds(core * pieces, pieces), pl.ds(0, PIECE)], 5, other, head)
     swap_back.start()
 
     def finish(h, block, halves, fresh):
@@ -351,10 +349,9 @@
     for block in range(blocks):
         for h, halves in zip(rest, rest_halves):
             finish(h, block, halves, False)
-        sums = jnp.sum(squares[pl.ds(block * BLOCK, BLOCK), :], axis=1, keepdims=True)
         for r in range(BLOCK // 128):
-            wide = jnp.broadcast_to(sums[r * 128 : (r + 1) * 128], (128, 128))
-            power_own[block, r : r + 1, :] = jnp.sum(jnp.where(eye, wide, 0.0), axis=0, keepdims=True)
+            turned = squares[pl.ds(block * BLOCK + r * 128, 128), :].T
+            power_own[block, r : r + 1, :] = jnp.sum(turned, axis=0, keepdims=True)
         power_all[block, head] = power_own[block]
         for step in range(1, head_n):
             remote(

time: 33.8 us -> 33.2 us (0.982)
  the two profiles are of different devices: /device:TPU:3 before, /device:TPU:2 now
where the time goes in v4:
time: 33.2 us; the launch traced here: 33.1 us
  Pallas kernels  32.1 us (97%)
  local copies, waits for them, and re-layouts  0.97 us (3%)
    pallas_call x1, Pallas kernels, local(): pl.pallas_call(functools.partial(mixer, dims), out_shape=jax.ShapeDtypeSt...  32.1 us
    unnamed x1, local copies, waits for them, and re-layouts  0.97 us

profile of v4, /device:TPU:2, one launch (start us, length us, event | category | flops | bytes accessed | tf_op | source)
XLA Modules:
  0.0 33.1 jit_solution(13792774422339628588)
XLA Ops:
  0.0 32.1 %mixer.1 = bf16[1024,512]{1,0:T(8,128)(2,1)S(1)} custom-call(bf16[64,1024]{1,0:T(8,128)(2,1)} %bitcast.2, bf16[64,1024]{1,0:T(8,128)(2,1)} %bitcast.3, bf16[1024,512]{1,0:T(8,128)(2,1)} %v_hbm.1, bf16[1024,512]{1,0:T(8,128)(2,1)} %wq_hbm.1, bf16[1024,512]{1,0:T(8,128)(2,1)} %wk_hbm.1, bf16[1024,512]{1,0:T(8,128)(2,1)} %wv_hbm.1, f32[4]{0:T(128)} %gain.1, ...), custom_call_target="tpu_custom_call" | custom-call | tf_op jit(solution)/shard_map/mixer/pallas_call | solution.py:400
  32.1 1.0 %copy.15 = bf16[1024,512]{1,0:T(8,128)(2,1)} copy(bf16[1024,512]{1,0:T(8,128)(2,1)S(1)} %mixer.1) | data formatting | bytes 2097152

commit v5 on v4

--- a/solution.py
+++ b/solution.py
@@ -123,8 +123,6 @@
 
     for copy in first_loads:
         copy.start()
-    for ref in (got, before, arrived):
-        ref[...] = jnp.zeros_like(ref)
     x, z = chip // z_n, lax.rem(chip, z_n)
     away = sorted(
         ((dx, dz) for dx in range(x_n) for dz in range(z_n) if dx or dz),
@@ -137,8 +135,6 @@
     greet(edge_mate, head)
     for step in range(1, head_n):
         greet(me, lax.rem(head + step, head_n))
-    for ref in (first_state, total):
-        ref[...] = jnp.zeros_like(ref)
 
     row_ids = lax.broadcasted_iota(jnp.int32, (ROWS, HD), 0)
     spots = row_ids + row_ids // PIECE * (SLOT - PIECE) - lax.broadcasted_iota(jnp.int32, (ROWS, HD), 1)
@@ -191,8 +187,6 @@
         remote(wk_hbm.at[pl.ds(tokens - W, W)], edge_k, 1, following, head),
         remote(wv_hbm.at[pl.ds(tokens - W, W)], edge_v, 2, following, head),
     ]
-    for copy in edges:
-        copy.start()
     swap_out.wait_recv()
     own = pl.ds(core * pieces, pieces)
     chip_sum[...] = total[own] + got[...]
@@ -203,6 +197,8 @@
         dst[chip] = src[chip]
 
     to_chips(chip_sum, gathered, 3)
+    for copy in edges:
+        copy.start()
 
     for copy in later_loads:
         copy.wait()
@@ -238,8 +234,10 @@
 
     spot = normal_row // PIECE * SLOT + normal_row % PIECE
 
+    used = lax.broadcasted_iota(jnp.int32, (PIECES, SLOT, HD), 1) < PIECE
+
     def state_halves(ref, h):
-        state = ref[pl.ds(h * PIECES, PIECES)].reshape(WIDE, HD)
+        state = jnp.where(used, ref[pl.ds(h * PIECES, PIECES)], 0.0).reshape(WIDE, HD)
         normal = jnp.concatenate(
             [jnp.broadcast_to(state[spot + i : spot + i + 1], (HD, HD)) for i in range(2)], axis=1
         )

time: 33.2 us -> 32.6 us (0.982)
  the two profiles are of different devices: /device:TPU:2 before, /device:TPU:1 now
where the time goes in v5:
time: 32.6 us; the launch traced here: 32 us
  Pallas kernels  31.1 us (95%)
  local copies, waits for them, and re-layouts  0.97 us (3%)
    pallas_call x1, Pallas kernels, local(): pl.pallas_call(functools.partial(mixer, dims), out_shape=jax.ShapeDtypeSt...  31.1 us
    unnamed x1, local copies, waits for them, and re-layouts  0.97 us

profile of v5, /device:TPU:1, one launch (start us, length us, event | category | flops | bytes accessed | tf_op | source)
XLA Modules:
  0.0 32.0 jit_solution(12607255131011712272)
XLA Ops:
  0.0 31.1 %mixer.1 = bf16[1024,512]{1,0:T(8,128)(2,1)S(1)} custom-call(bf16[64,1024]{1,0:T(8,128)(2,1)} %bitcast.2, bf16[64,1024]{1,0:T(8,128)(2,1)} %bitcast.3, bf16[1024,512]{1,0:T(8,128)(2,1)} %v_hbm.1, bf16[1024,512]{1,0:T(8,128)(2,1)} %wq_hbm.1, bf16[1024,512]{1,0:T(8,128)(2,1)} %wk_hbm.1, bf16[1024,512]{1,0:T(8,128)(2,1)} %wv_hbm.1, f32[4]{0:T(128)} %gain.1, ...), custom_call_target="tpu_custom_call" | custom-call | tf_op jit(solution)/shard_map/mixer/pallas_call | solution.py:398
  31.1 1.0 %copy.15 = bf16[1024,512]{1,0:T(8,128)(2,1)} copy(bf16[1024,512]{1,0:T(8,128)(2,1)S(1)} %mixer.1) | data formatting | bytes 2097152

commit v6 on v5

--- a/solution.py
+++ b/solution.py
@@ -191,8 +191,11 @@
     own = pl.ds(core * pieces, pieces)
     chip_sum[...] = total[own] + got[...]
 
+    by_z = sorted(away, key=lambda d: (-min(d[1], z_n - d[1]), -min(d[0], x_n - d[0])))
+    by_z = [lax.rem(x + dx, x_n) * z_n + lax.rem(z + dz, z_n) for dx, dz in by_z]
+
     def to_chips(src, dst, index):
-        for there in others:
+        for there in by_z:
             remote(src.at[there, pl.ds(0, PIECE)], dst.at[chip, pl.ds(0, PIECE)], index, 2 * there + core, head).start()
         dst[chip] = src[chip]
 
@@ -349,21 +352,18 @@
             finish(h, block, halves, False)
         for r in range(BLOCK // 128):
             turned = squares[pl.ds(block * BLOCK + r * 128, 128), :].T
-            power_own[block, r : r + 1, :] = jnp.sum(turned, axis=0, keepdims=True)
-        power_all[block, head] = power_own[block]
-        for step in range(1, head_n):
-            remote(
-                power_own.at[block], power_all.at[block, head], 6 + block, me, lax.rem(head + step, head_n)
-            ).start()
-
-    for block in range(blocks):
-        settle(power_all.at[block], head_n - 1, recv_sem.at[6 + block], BLOCK // 128)
-        power = jnp.sum(power_all[block], axis=0) * (1.0 / (heads * head_n * HD))
-        factor = lax.rsqrt(power + EPS)
-        for r in range(BLOCK // 128):
-            some = pl.ds(block * BLOCK + r * 128, 128)
-            column = jnp.broadcast_to(factor[r : r + 1], (128, 128)).T
-            out[some, :] = (window[some, :] * jnp.concatenate([column] * heads, axis=1)).astype(BF16)
+            q = block * BLOCK // 128 + r
+            power_own[q : q + 1, :] = jnp.sum(turned, axis=0, keepdims=True)
+    power_all[head] = power_own[...]
+    for step in range(1, head_n):
+        remote(power_own, power_all.at[head], 6, me, lax.rem(head + step, head_n)).start()
+
+    settle(power_all, head_n - 1, recv_sem.at[6], tokens // 128)
+    factor = lax.rsqrt(jnp.sum(power_all[...], axis=0) * (1.0 / (heads * head_n * HD)) + EPS)
+    for r in range(tokens // 128):
+        some = pl.ds(r * 128, 128)
+        column = jnp.broadcast_to(factor[r : r + 1], (128, 128)).T
+        out[some, :] = (window[some, :] * jnp.concatenate([column] * heads, axis=1)).astype(BF16)
 
     @pl.when(chip == 0)
     def _():
@@ -376,8 +376,7 @@
 
     settle(gathered, chips - 1, send_sem.at[3])
     settle(arrived, chips - 1, send_sem.at[4])
-    for block in range(blocks):
-        settle(power_all.at[block], head_n - 1, send_sem.at[6 + block], BLOCK // 128)
+    settle(power_all, head_n - 1, send_sem.at[6], tokens // 128)
 
 
 def solution(mesh):
@@ -419,8 +418,8 @@
                 vm((heads, tokens, 2 * HD), F32),
                 vm((tokens, width), F32),
                 vm((heads, tokens, WIDE), BF16),
-                vm((blocks, BLOCK // 128, 128), F32),
-                vm((blocks, head_n, BLOCK // 128, 128), F32),
+                vm((tokens // 128, 128), F32),
+                vm((head_n, tokens // 128, 128), F32),
                 vm((tokens, HD), F32),
                 pltpu.SemaphoreType.DMA((12,)),
                 pltpu.SemaphoreType.DMA((6 + blocks,)),

time: 32.6 us -> 32.5 us (level)
  no operation moved by 1% of the time
where the time goes in v6:
time: 32.5 us; the launch traced here: 32.1 us
  Pallas kernels  31.1 us (96%)
  local copies, waits for them, and re-layouts  0.97 us (3%)
    pallas_call x1, Pallas kernels, local(): pl.pallas_call(functools.partial(mixer, dims), out_shape=jax.ShapeDtypeSt...  31.1 us
    unnamed x1, local copies, waits for them, and re-layouts  0.97 us

profile of v6, /device:TPU:1, one launch (start us, length us, event | category | flops | bytes accessed | tf_op | source)
XLA Modules:
  0.0 32.1 jit_solution(17685480082659969950)
XLA Ops:
  0.0 31.1 %mixer.1 = bf16[1024,512]{1,0:T(8,128)(2,1)S(1)} custom-call(bf16[64,1024]{1,0:T(8,128)(2,1)} %bitcast.2, bf16[64,1024]{1,0:T(8,128)(2,1)} %bitcast.3, bf16[1024,512]{1,0:T(8,128)(2,1)} %v_hbm.1, bf16[1024,512]{1,0:T(8,128)(2,1)} %wq_hbm.1, bf16[1024,512]{1,0:T(8,128)(2,1)} %wk_hbm.1, bf16[1024,512]{1,0:T(8,128)(2,1)} %wv_hbm.1, f32[4]{0:T(128)} %gain.1, ...), custom_call_target="tpu_custom_call" | custom-call | tf_op jit(solution)/shard_map/mixer/pallas_call | solution.py:397
  31.2 1.0 %copy.15 = bf16[1024,512]{1,0:T(8,128)(2,1)} copy(bf16[1024,512]{1,0:T(8,128)(2,1)S(1)} %mixer.1) | data formatting | bytes 2097152
